TPU v7x, 32 devices: a whole 2x2x4 slice. The times are simulated.
32 devices in a mesh: ctx: 32 (over z, y, x, core).
Axes of the slice: x: 2, y: 2, z: 4, core: 2. Of those that a mesh axis runs over, the one named last changes fastest.
Arguments:
- queries: bfloat16 [4096, 512], P('ctx'), may hold values from -6 to 6
- keys: bfloat16 [4096, 512], P('ctx'), may hold values from -6 to 6
- values: bfloat16 [4096, 512], P('ctx'), may hold values from -6 to 6
- out_weight: bfloat16 [4096, 512], P('ctx'), may hold values from -0.25 to 0.25
- cotangent: bfloat16 [4096, 4096], P('ctx'), may hold values from -6 to 6
Outputs:
- mixed: bfloat16 [4096, 4096], P('ctx')
- query_gradient: bfloat16 [4096, 512], P('ctx')
- key_gradient: bfloat16 [4096, 512], P('ctx')
- value_gradient: bfloat16 [4096, 512], P('ctx')
- weight_grad: float32 [4096, 512], P('ctx')
All inputs are finite; a program needn't handle non-finite values.
Results may differ from a plain program's by a relative error of at most 0.014.
Values may be sent and summed in bfloat16 or wider, within the bound.
A program may use at most 320 MiB of HBM per device.

v0:
```python
import jax
import jax.numpy as jnp
from jax import lax
from jax.sharding import PartitionSpec as P

HEADS = 4
HEAD = 128


def carried_in(value, axis, combine, identity):
    size, index = (lax.axis_size(axis), lax.axis_index(axis))
    everything = lax.all_gather(value, axis)
    start = jnp.broadcast_to(jnp.asarray(identity, value.dtype), value.shape)

    def step(k, before):
        reached = k < index
        new = combine(before, everything[k])
        return jnp.where(reached, new, before)

    return lax.fori_loop(0, size, step, start)


def carried_in_2(value, axis, join, neutral):
    count = lax.axis_size(axis)
    place = lax.axis_index(axis)
    ahead = count - 1 - place
    gathered = lax.all_gather(value.astype(jnp.bfloat16), axis)
    state = jnp.zeros_like(value) + jnp.asarray(neutral, value.dtype)

    def one(step, state):
        source = count - 1 - step
        return join(state, lax.dynamic_index_in_dim(gathered, source, 0, False).astype(value.dtype))

    return lax.fori_loop(0, ahead, one, state)


def combine_sum(earlier, later):
    return jax.tree.map(jnp.add, earlier, later)


def body(queries, keys, values, out_weight, cotangent):
    tok_count = queries.shape[0]
    offset = lax.axis_index("ctx") * tok_count
    positions = offset + jnp.arange(tok_count, dtype=jnp.int32)
    position_scale = lax.rsqrt(HEAD * (positions + 1).astype(jnp.float32))
    head_shape = (tok_count, HEADS, HEAD)
    head_queries = queries.reshape(head_shape)
    head_keys = keys.reshape(head_shape)
    head_values = values.reshape(head_shape)
    full_weight = lax.all_gather(out_weight, "ctx", axis=0, tiled=True)
    grad_attended = jnp.dot(cotangent, full_weight, preferred_element_type=jnp.float32)
    scaled_grad = (grad_attended * position_scale[:, None]).astype(jnp.bfloat16)
    head_gradient = scaled_grad.reshape(head_shape)
    local_keys = jnp.einsum(
        "ixj,ixg->xjg", head_keys, head_values, preferred_element_type=jnp.float32
    )
    local_grads = jnp.einsum(
        "ixj,ixg->xjg", head_queries, head_gradient, preferred_element_type=jnp.float32
    )
    zero_state = jnp.zeros_like(local_keys)
    earlier_keys = carried_in(local_keys, "ctx", combine_sum, zero_state)
    later_grads = carried_in_2(local_grads, "ctx", combine_sum, zero_state)
    prefix_key_state = earlier_keys.astype(jnp.bfloat16)
    state_gradient = later_grads.astype(jnp.bfloat16)
    row_index = jnp.arange(tok_count, dtype=jnp.int32)
    causal = (row_index[:, None] >= row_index[None, :])[None]
    scores = jnp.einsum("shd,thd->hst", head_queries, head_keys, preferred_element_type=jnp.float32)
    masked_scores = jnp.where(causal, scores, 0.0).astype(jnp.bfloat16)
    local_part = jnp.einsum(
        "kun,nkr->ukr", masked_scores, head_values, preferred_element_type=jnp.float32
    )
    carried_over = jnp.einsum(
        "mqw,qwi->mqi", head_queries, prefix_key_state, preferred_element_type=jnp.float32
    )
    attended = (
        ((local_part + carried_over) * position_scale[:, None, None])
        .astype(jnp.bfloat16)
        .reshape(tok_count, -1)
    )
    mixed = lax.dot_general(
        attended, full_weight, (((1,), (1,)), ((), ())), preferred_element_type=jnp.float32
    ).astype(jnp.bfloat16)
    grad_scores = jnp.einsum(
        "shd,thd->hst", head_gradient, head_values, preferred_element_type=jnp.float32
    )
    masked_gradient = jnp.where(causal, grad_scores, 0.0).astype(jnp.bfloat16)
    query_gradient = jnp.einsum(
        "kun,nkr->ukr", masked_gradient, head_keys, preferred_element_type=jnp.float32
    )
    query_gradient = query_gradient + jnp.einsum(
        "riq,ipq->rip", head_gradient, prefix_key_state, preferred_element_type=jnp.float32
    )
    key_gradient = jnp.einsum(
        "olf,loy->foy", masked_gradient, head_queries, preferred_element_type=jnp.float32
    )
    key_gradient = key_gradient + jnp.einsum(
        "rwd,wed->rwe", head_values, state_gradient, preferred_element_type=jnp.float32
    )
    value_gradient = jnp.einsum(
        "olf,loy->foy", masked_scores, head_gradient, preferred_element_type=jnp.float32
    )
    value_gradient = value_gradient + jnp.einsum(
        "pyd,yda->pya", head_keys, state_gradient, preferred_element_type=jnp.float32
    )
    flat_shape = (tok_count, -1)
    query_gradient = query_gradient.reshape(flat_shape).astype(jnp.bfloat16)
    key_gradient = key_gradient.reshape(flat_shape).astype(jnp.bfloat16)
    value_gradient = value_gradient.reshape(flat_shape).astype(jnp.bfloat16)
    weight_term = lax.dot_general(
        cotangent, attended, (((0,), (0,)), ((), ())), preferred_element_type=jnp.float32
    )
    weight_grad = lax.psum_scatter(weight_term, "ctx", scatter_dimension=0, tiled=True)
    return (mixed, query_gradient, key_gradient, value_gradient, weight_grad)


def solution(mesh):
    return jax.shard_map(
        body,
        mesh=mesh,
        in_specs=(P("ctx", None), P("ctx", None), P("ctx", None), P("ctx", None), P("ctx", None)),
        out_specs=(P("ctx", None), P("ctx", None), P("ctx", None), P("ctx", None), P("ctx", None)),
        check_vma=False,
    )
```

profile of v0, /device:TPU:0, one launch (start us, length us, event | category | flops | bytes accessed | tf_op | source)
XLA Modules:
  0.0 377.1 jit_solution(10598600412393620999)
XLA Ops:
  8.0 1.0 copy.102
  9.0 1.8 fusion.15
  10.9 1.2 fusion.7
  12.1 1.1 convolution_bitcast_fusion.6
  13.2 62.4 %all-gather.6.cloned.1.call-done = bf16[4096,512]{1,0:T(8,128)(2,1)} async-done(((bf16[128,512]{1,0:T(8,128)(2,1)}), bf16[4096,512]{1,0:T(8,128)(2,1)}) %all-gather.6.cloned.1.call-update) | async-done | bytes 4194320 | tf_op jit(solution)/shard_map/all_gather | solution.py:50
  75.7 2.9 fusion.10
  79.7 75.4 %all-gather.8.cloned.1.call-done = f32[128,128,128]{2,1,0:T(8,128)} async-done(((f32[4,128,128]{2,1,0:T(8,128)}), f32[128,128,128]{2,1,0:T(8,128)}) %all-gather.8.cloned.1.call-update) | async-done | bytes 8388624 | tf_op jit(solution)/shard_map/all_gather | solution.py:12
  155.1 34.1 %while.27 = (s32[]{:T(128)}, f32[4,128,128]{2,1,0:T(8,128)S(1)}, s32[]{:T(128)}, f32[32,4,128,128]{3,2,1,0:T(8,128)}, s32[]{:T(128)}, /*index=5*/s32[]{:T(128)}) while((s32[]{:T(128)}, f32[4,128,128]{2,1,0:T(8,128)S(1)}, s32[]{:T(128)}, f32[32,4,128,128]{3,2,1,0:T(8,128)}, s32[]{:T(128)}, /*index=5*/s32[]{:T(128)}) %tuple.74), condition=%wide.region_1.2_spmd.clone, body=%wide.region_0.1_spmd.clone.sunk | while | flops 196612 | bytes 786533 | solution.py:20
  155.1 1.0 add_select_fusion.2
  156.2 1.0 add_select_fusion.2
  157.3 1.0 add_select_fusion.2
  158.3 1.0 add_select_fusion.2
  159.4 1.0 add_select_fusion.2
  160.4 1.0 add_select_fusion.2
  161.5 1.0 add_select_fusion.2
  162.6 1.0 add_select_fusion.2
  163.6 1.0 add_select_fusion.2
  164.7 1.0 add_select_fusion.2
  165.8 1.0 add_select_fusion.2
  166.8 1.0 add_select_fusion.2
  167.9 1.0 add_select_fusion.2
  169.0 1.0 add_select_fusion.2
  170.0 1.0 add_select_fusion.2
  171.1 1.0 add_select_fusion.2
  172.2 1.0 add_select_fusion.2
  173.2 1.0 add_select_fusion.2
  174.3 1.0 add_select_fusion.2
  175.4 1.0 add_select_fusion.2
  176.4 1.0 add_select_fusion.2
  177.5 1.0 add_select_fusion.2
  178.6 1.0 add_select_fusion.2
  179.6 1.0 add_select_fusion.2
  180.7 1.0 add_select_fusion.2
  181.7 1.1 add_select_fusion.2
  182.9 1.0 add_select_fusion.2
  183.9 1.0 add_select_fusion.2
  185.0 1.0 add_select_fusion.2
  186.1 1.0 add_select_fusion.2
  187.1 1.0 add_select_fusion.2
  188.2 1.0 add_select_fusion.2
  189.5 4.5 %convolution_bitcast_fusion = f32[4096,512]{0,1:T(8,128)} fusion(bf16[128,512]{0,1:T(8,128)(2,1)S(1)} %bitcast.125, bf16[128,4096]{1,0:T(8,128)(2,1)S(1)} %copy-done), kind=kOutput, calls=%fused_computation.2 | convolution fusion | flops 536870912 | bytes 9568256 | tf_op jit(solution)/shard_map/dot_general | solution.py:109
  196.4 22.8 %all-gather.10.cloned.1.call-done = bf16[128,128,128]{2,1,0:T(8,128)(2,1)} async-done(((bf16[4,128,128]{2,1,0:T(8,128)(2,1)}), bf16[128,128,128]{2,1,0:T(8,128)(2,1)}) %all-gather.10.cloned.1.call-update) | async-done | bytes 4194320 | tf_op jit(solution)/shard_map/all_gather | solution.py:27
  219.2 30.6 %while.26 = (s32[]{:T(128)}, f32[4,128,128]{2,1,0:T(8,128)S(1)}, s32[]{:T(128)}, bf16[32,4,128,128]{3,2,1,0:T(8,128)(2,1)}, s32[]{:T(128)}, /*index=5*/s32[]{:T(128)}, s32[]{:T(128)}, s32[]{:T(128)}) while((s32[]{:T(128)}, f32[4,128,128]{2,1,0:T(8,128)S(1)}, s32[]{:T(128)}, bf16[32,4,128,128]{3,2,1,0:T(8,128)(2,1)}, s32[]{:T(128)}, ...), condition=%wide.region_3.4_spmd, body=%wide.region_2.3_spmd.sunk | while | flops 131078 | bytes 655503 | solution.py:34
  225.2 1.0 convert_add_fusion.2
  233.1 1.0 convert_add_fusion.2
  252.1 4.7 %convolution_convert_fusion = bf16[128,4096]{1,0:T(8,128)(2,1)} fusion(bf16[128,512]{0,1:T(8,128)(2,1)S(1)} %bitcast.126, bf16[4096,512]{1,0:T(8,128)(2,1)} %all-gather.6.cloned.1.call-done), kind=kOutput, calls=%fused_computation.3 | convolution fusion | flops 537395200 | bytes 5373952 | tf_op jit(solution)/shard_map/dot_general | solution.py:80
  256.9 111.9 %reduce-scatter.2.cloned.1.call-done = f32[128,512]{0,1:T(8,128)} async-done(((f32[4096,512]{0,1:T(8,128)}), f32[128,512]{0,1:T(8,128)}) %reduce-scatter.2.cloned.1.call-update) | async-done | bytes 262160 | tf_op jit(solution)/shard_map/reduce_scatter | solution.py:112
  368.8 1.8 copy.55
  (63 shorter events, 34.9 us)
Async XLA Ops:
  7.2 68.5 %copy-start = (bf16[128,4096]{1,0:T(8,128)(2,1)S(1)}, bf16[128,4096]{1,0:T(8,128)(2,1)}, u32[]{:S(2)}) copy-start(bf16[128,4096]{1,0:T(8,128)(2,1)} %param.13) | copy-start | bytes 3145732
  7.2 71.5 %copy-start.1 = (bf16[128,512]{1,0:T(8,128)(2,1)S(1)}, bf16[128,512]{1,0:T(8,128)(2,1)}, u32[]{:S(2)}) copy-start(bf16[128,512]{1,0:T(8,128)(2,1)} %param.9) | copy-start | bytes 393220
  7.2 68.5 %all-gather.6.cloned.1.call-start = ((), (), s32[]{:S(2)}) async-start(), calls=%async_computation.1 | async-start | bytes 4325376 | tf_op jit(solution)/shard_map/all_gather | solution.py:50
  7.9 147.2 %all-gather.8.cloned.1.call-start = ((), (), s32[]{:S(2)}) async-start(), calls=%async_computation.3 | async-start | bytes 8650752 | tf_op jit(solution)/shard_map/all_gather | solution.py:12
  10.8 208.4 %all-gather.10.cloned.1.call-start = ((), (), s32[]{:S(2)}) async-start(), calls=%async_computation.4 | async-start | bytes 4325376 | tf_op jit(solution)/shard_map/all_gather | solution.py:27
  79.7 289.1 %reduce-scatter.2.cloned.1.call-start = ((), (), s32[]{:S(2)}) async-start(), calls=%async_computation.2 | async-start | bytes 8650752 | tf_op jit(solution)/shard_map/reduce_scatter | solution.py:112
  194.0 0.9 copy-start.2
  194.0 57.1 %copy-start.3 = (bf16[128,512]{1,0:T(8,128)(2,1)S(1)}, bf16[128,512]{1,0:T(8,128)(2,1)}, u32[]{:S(2)}) copy-start(bf16[128,512]{1,0:T(8,128)(2,1)} %param.10) | copy-start | bytes 393220
Sparse Core Ops, SparseCore 0:
  10.9 64.7 all-gather.5
  79.1 75.9 all-gather.7
  158.6 60.6 all-gather.9
  221.4 147.3 reduce-scatter.1
where the time goes:
time: 379 us; the launch traced here: 377 us
  waiting for transfers between devices  273 us (72%)
  other arithmetic  63.3 us (17%)
  matrix products  18.1 us (5%)
  between operations  13.9 us (4%)
  local copies, waits for them, and re-layouts  6.91 us (2%)
    reduce_scatter x1, waiting for transfers between devices, body(): lax.psum_scatter(weight_term, 'ctx', scatter_dimension=0, tiled=True)  112 us
    all_gather x1, waiting for transfers between devices, carried_in(): everything = lax.all_gather(value, axis)  75.4 us
    all_gather x1, waiting for transfers between devices, body(): full_weight = lax.all_gather(out_weight, 'ctx', axis=0, tiled=True)  62.4 us
    select_n x32, other arithmetic, step(): return jnp.where(reached, new, before)  33.4 us
    add x31, other arithmetic, combine_sum(): return jax.tree.map(jnp.add, earlier, later)  29.9 us
    all_gather x1, waiting for transfers between devices, carried_in_2(): gathered = lax.all_gather(value.astype(jnp.bfloat16), axis)  22.8 us
  transfers between devices with their start and end apart: 4, of which 4 were waited for; matrix products, arithmetic and copies ran while one was open for 23% of the time, Pallas kernels for 0%

commit v1 on v0

v1 whole, which is shorter than its diff:
```python
import functools

import jax
import jax.numpy as jnp
from jax import lax
from jax.experimental import pallas as pl
from jax.experimental.pallas import tpu as pltpu
from jax.sharding import PartitionSpec as P

HEADS = 4
HEAD = 128
GROUP = 8
F32 = jnp.float32
BF16 = jnp.bfloat16
MESH = pl.DeviceIdType.MESH


def dot(x, y, dims):
    return lax.dot_general(x, y, (dims, ((), ())), preferred_element_type=F32)


NN = ((1,), (0,))
NT = ((1,), (1,))
TN = ((0,), (0,))


def kernel(
    planes,
    q_ref, k_ref, v_ref, w_ref, cot_ref,
    mixed_ref, dq_ref, dk_ref, dv_ref, wg_ref,
    full_w, part, from_sib, summed, from_diag, from_x, from_y, to_plane, from_plane, own_sum,
    scores, local_part, att, grad,
    piece_out, piece_in, total_out, totals, prefix_out, state,
    p1_send, p1_recv, p2_send, p2_recv, p3_send, p3_recv,
    z_send, z_recv, x_send, x_recv, y_send, y_recv, g_send, g_recv, s_send, s_recv,
    rs_send, rs_recv, rd_send, rd_recv, rx_send, rx_recv, ry_send, ry_recv, rz_send, rz_recv,
):
    tokens = q_ref.shape[0]
    rows = w_ref.shape[0]
    width = GROUP * rows
    me = lax.axis_index("ctx")
    plane = lax.div(me, GROUP)
    member = lax.rem(me, GROUP)
    core = lax.rem(member, 2)
    quad = lax.div(member, 2)
    quad_x = lax.rem(quad, 2)
    quad_y = lax.div(quad, 2)
    to_x = 1 - 2 * quad_x
    to_y = 2 - 4 * quad_y
    col_x = quad + to_x
    col_y = quad + to_y
    col_d = 3 - quad
    x_dev = me + 2 * to_x
    y_dev = me + 2 * to_y
    sib = me + 1 - 2 * core
    other = 1 - core

    def mate(r):
        return lax.rem(member + r, GROUP)

    def mate_dev(r):
        return plane * GROUP + mate(r)

    def plane_at(d):
        return lax.rem(plane + d, planes)

    def plane_before(d):
        return lax.rem(plane + planes - d, planes)

    def plane_dev(d):
        return plane_at(d) * GROUP + member

    def copy(src, dst, send, recv, device):
        return pltpu.make_async_remote_copy(
            src_ref=src, dst_ref=dst, send_sem=send, recv_sem=recv,
            device_id=(device,), device_id_type=MESH,
        )

    sent = []

    def start(c):
        c.start()
        sent.append(c)

    barrier = pltpu.get_barrier_semaphore()
    for r in range(1, GROUP):
        pl.semaphore_signal(barrier, inc=1, device_id=(mate_dev(r),), device_id_type=MESH)
    for d in range(1, planes):
        pl.semaphore_signal(barrier, inc=1, device_id=(plane_dev(d),), device_id_type=MESH)

    def head(ref, h):
        return ref[:, h * HEAD:(h + 1) * HEAD]

    def pieces(way, left, right):
        for h in range(HEADS):
            outer = dot(head(left, h), head(right, h), TN).astype(BF16)
            piece_out[way, 2 * h:2 * h + 2] = outer.reshape(2, HEAD // 2, HEAD)

    def piece_copy(way, r):
        return copy(piece_out.at[way, mate(r)], piece_in.at[way, member],
                    p1_send.at[way, r], p1_recv.at[way, r], mate_dev(r))

    def send_pieces(way):
        for r in range(1, GROUP):
            start(piece_copy(way, r))
        piece_in[way, member] = piece_out[way, member]

    def total_copy(way, d):
        return copy(total_out.at[way], totals.at[way, plane],
                    p2_send.at[way, d], p2_recv.at[way, d], plane_dev(d))

    def send_totals(way):
        for r in range(1, GROUP):
            piece_copy(way, r).wait_recv()
        total = piece_in[way, 0].astype(F32)
        for j in range(1, GROUP):
            total = total + piece_in[way, j].astype(F32)
        total_out[way] = total
        totals[way, plane] = total
        for d in range(1, planes):
            start(total_copy(way, d))

    def prefix_copy(way, r):
        return copy(prefix_out.at[way, mate(r)], state.at[way, member],
                    p3_send.at[way, r], p3_recv.at[way, r], mate_dev(r))

    def send_prefixes(way):
        for d in range(1, planes):
            total_copy(way, d).wait_recv()
        run = jnp.zeros((HEAD // 2, HEAD), F32)
        for i in range(planes):
            counts = (i < plane) if way == 0 else (i > plane)
            run = run + jnp.where(counts, totals[way, i], 0.0)
        for j in (range(GROUP) if way == 0 else range(GROUP - 1, -1, -1)):
            prefix_out[way, j] = run.astype(BF16)
            run = run + piece_in[way, j].astype(F32)
        for r in range(1, GROUP):
            start(prefix_copy(way, r))
        state[way, member] = prefix_out[way, member]

    def wait_state(way):
        for r in range(1, GROUP):
            prefix_copy(way, r).wait_recv()

    def state_of(way, h):
        return state[way, 2 * h:2 * h + 2].reshape(HEAD, HEAD)

    def z_copy(d):
        return copy(w_ref, full_w.at[plane, quad, core], z_send.at[d], z_recv.at[d], plane_dev(d))

    def block(d, col):
        return full_w.at[plane_before(d), col, core]

    def move(d, col, sems, device, first=False):
        send, recv = sems
        return copy(w_ref if first else block(d, col), block(d, col), send, recv, device)

    def x_copy(d, first=False):
        return move(d, quad, (x_send.at[d], x_recv.at[d]), x_dev, first)

    def y_copy(d, first=False):
        return move(d, quad, (y_send.at[d], y_recv.at[d]), y_dev, first)

    def diag_copy(d):
        if d % 2 == 0:
            return move(d, col_y, (g_send.at[d], g_recv.at[d]), x_dev)
        return move(d, col_x, (g_send.at[d], g_recv.at[d]), y_dev)

    def sib_copy(d, i, first=False):
        col = (quad, col_x, col_y, col_d)[i]
        return move(d, col, (s_send.at[d, i], s_recv.at[d, i]), sib, first)

    def spread(d):
        if d:
            z_copy(d).wait_recv()
        start(x_copy(d, d == 0))
        start(y_copy(d, d == 0))
        start(sib_copy(d, 0, d == 0))

    def pass_on(d):
        x_copy(d).wait_recv()
        if d % 2:
            start(diag_copy(d))
        start(sib_copy(d, 1))
        y_copy(d).wait_recv()
        if d % 2 == 0:
            start(diag_copy(d))
        start(sib_copy(d, 2))

    def pass_diag(d):
        diag_copy(d).wait_recv()
        start(sib_copy(d, 3))

    def rs_copy(d):
        return copy(part.at[d, :, other], from_sib.at[d], rs_send.at[d], rs_recv.at[d], sib)

    def reduce_1(d):
        columns = pl.ds(pl.multiple_of(plane_at(d) * width, 128), width)
        term = dot(cot_ref[:, columns], att[...], TN).astype(BF16)
        part[d] = term.reshape(4, 2, rows, term.shape[-1])
        start(rs_copy(d))

    def rd_copy(d):
        return copy(summed.at[d, col_d], from_diag.at[d], rd_send.at[d], rd_recv.at[d],
                    y_dev if d % 2 else x_dev)

    def rx_copy(d):
        return copy(summed.at[d, col_x], from_x.at[d], rx_send.at[d], rx_recv.at[d], x_dev)

    def ry_copy(d):
        return copy(summed.at[d, col_y], from_y.at[d], ry_send.at[d], ry_recv.at[d], y_dev)

    def reduce_2(d):
        rs_copy(d).wait_recv()

        def add(col):
            pair = part[d, col, core].astype(F32) + from_sib[d, col].astype(F32)
            summed[d, col] = pair.astype(BF16)

        add(col_d)
        start(rd_copy(d))
        if d % 2:
            add(col_y)
            start(ry_copy(d))
            add(col_x)
        else:
            add(col_x)
            start(rx_copy(d))
            add(col_y)

    def reduce_3(d):
        rd_copy(d).wait_recv()
        col = col_x if d % 2 else col_y
        both = summed[d, col].astype(F32) + from_diag[d].astype(F32)
        summed[d, col] = both.astype(BF16)
        start(rx_copy(d) if d % 2 else ry_copy(d))

    def rz_copy(d):
        return copy(to_plane.at[d], from_plane.at[d], rz_send.at[d], rz_recv.at[d], plane_dev(d))

    def reduce_4(d):
        rx_copy(d).wait_recv()
        ry_copy(d).wait_recv()
        pair = part[d, quad, core].astype(F32) + from_sib[d, quad].astype(F32)
        total = pair + from_x[d].astype(F32) + from_y[d].astype(F32)
        if d:
            to_plane[d] = total.astype(BF16)
            start(rz_copy(d))
        else:
            own_sum[...] = total

    def reduce_5():
        total = own_sum[...]
        for d in range(1, planes):
            rz_copy(d).wait_recv()
            total = total + from_plane[d].astype(F32)
        wg_ref[...] = total

    targets = list(range(1, planes)) + [0]

    position = me * tokens + lax.broadcasted_iota(jnp.int32, (tokens, 1), 0)
    scale = lax.rsqrt(HEAD * (position + 1).astype(F32))
    causal = lax.broadcasted_iota(jnp.int32, (tokens, tokens), 0) >= lax.broadcasted_iota(
        jnp.int32, (tokens, tokens), 1
    )

    pieces(0, k_ref, v_ref)
    pl.semaphore_wait(barrier, GROUP - 1 + planes - 1)
    send_pieces(0)
    for d in range(1, planes):
        start(z_copy(d))
    spread(0)
    full_w[plane, quad, core] = w_ref[...]
    for h in range(HEADS):
        s = jnp.where(causal, dot(head(q_ref, h), head(k_ref, h), NT), 0.0).astype(BF16)
        scores[h] = s
        local_part[h] = dot(s, head(v_ref, h), NN)
    send_totals(0)
    spread(1)
    send_prefixes(0)
    for d in range(2, planes):
        spread(d)
    wait_state(0)
    for h in range(HEADS):
        a = (local_part[h] + dot(head(q_ref, h), state_of(0, h), NN)) * scale
        att[:, h * HEAD:(h + 1) * HEAD] = a.astype(BF16)
    for d in range(planes):
        pass_on(d)
        reduce_1(targets[d])
    for d in range(planes):
        pass_diag(d)
        reduce_2(targets[d])

    grad_acc = jnp.zeros(att.shape, F32)
    for d in range(planes):
        for i in range(4):
            sib_copy(d, i).wait_recv()
    for i in range(planes):
        w = full_w[i].reshape(width, w_ref.shape[1])
        grad_acc = grad_acc + dot(cot_ref[:, i * width:(i + 1) * width], w, NN)
    grad[...] = (grad_acc * scale).astype(BF16)
    pieces(1, q_ref, grad)
    send_pieces(1)
    for d in targets:
        reduce_3(d)
    send_totals(1)
    for i in range(planes // 2):
        w = full_w[i].reshape(width, w_ref.shape[1])
        mixed_ref[:, i * width:(i + 1) * width] = dot(att[...], w, NT).astype(BF16)
    send_prefixes(1)
    for d in targets:
        reduce_4(d)
    for i in range(planes // 2, planes):
        w = full_w[i].reshape(width, w_ref.shape[1])
        mixed_ref[:, i * width:(i + 1) * width] = dot(att[...], w, NT).astype(BF16)
    wait_state(1)
    for h in range(HEADS):
        cols = slice(h * HEAD, (h + 1) * HEAD)
        q, k, v, g = head(q_ref, h), head(k_ref, h), head(v_ref, h), head(grad, h)
        gs = jnp.where(causal, dot(g, v, NT), 0.0).astype(BF16)
        dq_ref[:, cols] = (dot(gs, k, NN) + dot(g, state_of(0, h), NT)).astype(BF16)
        dk_ref[:, cols] = (dot(gs, q, TN) + dot(v, state_of(1, h), NT)).astype(BF16)
        dv_ref[:, cols] = (dot(scores[h], g, TN) + dot(k, state_of(1, h), NN)).astype(BF16)
    reduce_5()
    for c in sent:
        c.wait_send()


def body(planes, queries, keys, values, out_weight, cotangent):
    tokens, hf = queries.shape
    rows = out_weight.shape[0]
    half = HEAD // 2
    dma = pltpu.SemaphoreType.DMA
    vmem = pl.BlockSpec(memory_space=pltpu.VMEM)
    blocks = pltpu.VMEM((planes, rows, hf), BF16)
    return pl.pallas_call(
        functools.partial(kernel, planes),
        out_shape=(
            jax.ShapeDtypeStruct(cotangent.shape, BF16),
            jax.ShapeDtypeStruct(queries.shape, BF16),
            jax.ShapeDtypeStruct(queries.shape, BF16),
            jax.ShapeDtypeStruct(queries.shape, BF16),
            jax.ShapeDtypeStruct(out_weight.shape, F32),
        ),
        in_specs=[vmem] * 5,
        out_specs=(vmem,) * 5,
        scratch_shapes=[
            pltpu.VMEM((planes, 4, 2, rows, hf), BF16),
            pltpu.VMEM((planes, 4, 2, rows, hf), BF16),
            pltpu.VMEM((planes, 4, rows, hf), BF16),
            pltpu.VMEM((planes, 4, rows, hf), BF16),
            blocks, blocks, blocks, blocks, blocks,
            pltpu.VMEM((rows, hf), F32),
            pltpu.VMEM((HEADS, tokens, tokens), BF16),
            pltpu.VMEM((HEADS, tokens, HEAD), F32),
            pltpu.VMEM((tokens, hf), BF16),
            pltpu.VMEM((tokens, hf), BF16),
            pltpu.VMEM((2, GROUP, half, HEAD), BF16),
            pltpu.VMEM((2, GROUP, half, HEAD), BF16),
            pltpu.VMEM((2, half, HEAD), F32),
            pltpu.VMEM((2, planes, half, HEAD), F32),
            pltpu.VMEM((2, GROUP, half, HEAD), BF16),
            pltpu.VMEM((2, GROUP, half, HEAD), BF16),
            dma((2, GROUP)), dma((2, GROUP)),
            dma((2, planes)), dma((2, planes)),
            dma((2, GROUP)), dma((2, GROUP)),
        ] + [dma((planes,))] * 8 + [dma((planes, 4))] * 2 + [dma((planes,))] * 10,
        compiler_params=pltpu.CompilerParams(
            collective_id=0, has_side_effects=True, vmem_limit_bytes=48 * 1024 * 1024
        ),
    )(queries, keys, values, out_weight, cotangent)


def solution(mesh):
    planes = mesh.shape["ctx"] // GROUP
    spec = P("ctx", None)
    return jax.shard_map(
        functools.partial(body, planes),
        mesh=mesh,
        in_specs=(spec,) * 5,
        out_specs=(spec,) * 5,
        check_vma=False,
    )
```

time: 379 us -> 76.1 us (0.20)
  waiting for transfers between devices: 273 us -> 0 us
  Pallas kernels: 0 us -> 66.8 us
  other arithmetic: 63.3 us -> 0 us
  matrix products: 18.1 us -> 0 us
  between operations: 13.9 us -> 0.66 us
    all_gather x3 -> x0, waiting for transfers between devices: 161 us -> none  [the longest x1 75.4 us: carried_in(): everything = lax.all_gather(value, axis)]
    reduce_scatter x1 -> x0, waiting for transfers between devices: 112 us -> none  [body(): lax.psum_scatter(weight_term, 'ctx', scatter_dimension=0, tiled=True)]
    pallas_call x0 -> x1, Pallas kernels: none -> 66.8 us  [body(): pl.pallas_call(functools.partial(kernel, planes), out_shape=(jax.ShapeDty...]
    select_n x32 -> x0, other arithmetic: 33.4 us -> none  [step(): return jnp.where(reached, new, before)]
    add x31 -> x0, other arithmetic: 29.9 us -> none  [combine_sum(): return jax.tree.map(jnp.add, earlier, later)]
    dot_general x15 -> x0, matrix products: 18.1 us -> none  [the longest x1 4.74 us: body(): lax.dot_general(attended, full_weight, (((1,), (1,)), ((), ())), preferre...]
    unnamed x12 -> x15, local copies, waits for them, and re-layouts: 4.99 us -> 8.47 us
  transfers between devices with their start and end apart: 4 -> 0, of which waited for: 4 -> 0; matrix products, arithmetic and copies ran while one was open for 23% -> 0% of each run, Pallas kernels for 0% -> 0%
where the time goes in v1:
time: 76.1 us; the launch traced here: 75.9 us
  Pallas kernels  66.8 us (88%)
  local copies, waits for them, and re-layouts  8.47 us (11%)
    pallas_call x1, Pallas kernels, body(): pl.pallas_call(functools.partial(kernel, planes), out_shape=(jax.ShapeDty...  66.8 us
    unnamed x15, local copies, waits for them, and re-layouts  8.47 us

profile of v1, /device:TPU:0, one launch (start us, length us, event | category | flops | bytes accessed | tf_op | source)
XLA Modules:
  0.0 75.9 jit_solution(11208315180353332637)
XLA Ops:
  0.6 0.0 copy-start
  0.6 1.2 %copy-done = bf16[128,4096]{1,0:T(8,128)(2,1)S(1)} copy-done((bf16[128,4096]{1,0:T(8,128)(2,1)S(1)}, bf16[128,4096]{1,0:T(8,128)(2,1)}, u32[]{:S(2)}) %copy-start) | copy-done | bytes 1048600
  1.9 0.0 copy-start.1
  1.9 0.9 %copy-done.1 = bf16[128,512]{1,0:T(8,128)(2,1)S(1)} copy-done((bf16[128,512]{1,0:T(8,128)(2,1)S(1)}, bf16[128,512]{1,0:T(8,128)(2,1)}, u32[]{:S(2)}) %copy-start.1) | copy-done | bytes 131096
  2.8 0.0 copy-start.2
  2.8 0.9 %copy-done.2 = bf16[128,512]{1,0:T(8,128)(2,1)S(1)} copy-done((bf16[128,512]{1,0:T(8,128)(2,1)S(1)}, bf16[128,512]{1,0:T(8,128)(2,1)}, u32[]{:S(2)}) %copy-start.2) | copy-done | bytes 131096
  3.7 0.0 copy-start.3
  3.7 0.9 %copy-done.3 = bf16[128,512]{1,0:T(8,128)(2,1)S(1)} copy-done((bf16[128,512]{1,0:T(8,128)(2,1)S(1)}, bf16[128,512]{1,0:T(8,128)(2,1)}, u32[]{:S(2)}) %copy-start.3) | copy-done | bytes 131096
  4.6 0.0 copy-start.4
  4.6 0.9 %copy-done.4 = bf16[128,512]{1,0:T(8,128)(2,1)S(1)} copy-done((bf16[128,512]{1,0:T(8,128)(2,1)S(1)}, bf16[128,512]{1,0:T(8,128)(2,1)}, u32[]{:S(2)}) %copy-start.4) | copy-done | bytes 131096
  5.5 66.8 %shard_map.92 = (bf16[128,4096]{1,0:T(8,128)(2,1)S(1)}, bf16[128,512]{1,0:T(8,128)(2,1)S(1)}, bf16[128,512]{1,0:T(8,128)(2,1)S(1)}, bf16[128,512]{1,0:T(8,128)(2,1)S(1)}, f32[128,512]{1,0:T(8,128)S(1)}) custom-call(bf16[128,512]{1,0:T(8,128)(2,1)S(1)} %copy-done.1, bf16[128,512]{1,0:T(8,128)(2,1)S(1)} %copy-done.2, bf16[128,512]{1,0:T(8,128)(2,1)S(1)} %copy-done.3, ...), custom_call_target="tpu_custom_call" | custom-call | tf_op jit(solution)/shard_map/pallas_call | solution.py:336
  72.3 1.0 %copy.15 = bf16[128,4096]{1,0:T(8,128)(2,1)} copy(bf16[128,4096]{1,0:T(8,128)(2,1)S(1)} %get-tuple-element.10) | data formatting | bytes 2097152
  73.2 0.7 copy.16
  73.9 0.7 copy.17
  74.5 0.7 copy.18
  75.2 0.7 copy.19
Async XLA Ops:
  0.6 1.2 %copy-start = (bf16[128,4096]{1,0:T(8,128)(2,1)S(1)}, bf16[128,4096]{1,0:T(8,128)(2,1)}, u32[]{:S(2)}) copy-start(bf16[128,4096]{1,0:T(8,128)(2,1)} %cot_ref.1) | copy-start | bytes 3145732
  1.9 0.9 %copy-start.1 = (bf16[128,512]{1,0:T(8,128)(2,1)S(1)}, bf16[128,512]{1,0:T(8,128)(2,1)}, u32[]{:S(2)}) copy-start(bf16[128,512]{1,0:T(8,128)(2,1)} %q_ref.1) | copy-start | bytes 393220
  2.8 0.9 %copy-start.2 = (bf16[128,512]{1,0:T(8,128)(2,1)S(1)}, bf16[128,512]{1,0:T(8,128)(2,1)}, u32[]{:S(2)}) copy-start(bf16[128,512]{1,0:T(8,128)(2,1)} %k_ref.1) | copy-start | bytes 393220
  3.7 0.9 %copy-start.3 = (bf16[128,512]{1,0:T(8,128)(2,1)S(1)}, bf16[128,512]{1,0:T(8,128)(2,1)}, u32[]{:S(2)}) copy-start(bf16[128,512]{1,0:T(8,128)(2,1)} %v_ref.1) | copy-start | bytes 393220
  4.6 0.9 %copy-start.4 = (bf16[128,512]{1,0:T(8,128)(2,1)S(1)}, bf16[128,512]{1,0:T(8,128)(2,1)}, u32[]{:S(2)}) copy-start(bf16[128,512]{1,0:T(8,128)(2,1)} %w_ref.1) | copy-start | bytes 393220

commit v2 on v1

--- a/solution.py
+++ b/solution.py
@@ -26,8 +26,9 @@
 
 def kernel(
     planes,
-    q_ref, k_ref, v_ref, w_ref, cot_ref,
+    q_hbm, k_hbm, v_hbm, w_ref, cot_hbm,
     mixed_ref, dq_ref, dk_ref, dv_ref, wg_ref,
+    q_ref, k_ref, v_ref, cot_ref, load,
     full_w, part, from_sib, summed, from_diag, from_x, from_y, to_plane, from_plane, own_sum,
     scores, local_part, att, grad,
     piece_out, piece_in, total_out, totals, prefix_out, state,
@@ -82,6 +83,16 @@
         c.start()
         sent.append(c)
 
+    loads = [
+        pltpu.make_async_copy(src, dst, load.at[i])
+        for i, (src, dst) in enumerate((
+            (k_hbm, k_ref), (v_hbm, v_ref), (q_hbm, q_ref),
+            (w_ref, full_w.at[plane, quad, core]), (cot_hbm, cot_ref),
+        ))
+    ]
+    for c in loads:
+        c.start()
+
     barrier = pltpu.get_barrier_semaphore()
     for r in range(1, GROUP):
         pl.semaphore_signal(barrier, inc=1, device_id=(mate_dev(r),), device_id_type=MESH)
@@ -264,55 +275,69 @@
         jnp.int32, (tokens, tokens), 1
     )
 
+    loads[0].wait()
+    loads[1].wait()
     pieces(0, k_ref, v_ref)
     pl.semaphore_wait(barrier, GROUP - 1 + planes - 1)
     send_pieces(0)
-    for d in range(1, planes):
-        start(z_copy(d))
+    start(z_copy(1))
     spread(0)
-    full_w[plane, quad, core] = w_ref[...]
+    loads[2].wait()
     for h in range(HEADS):
         s = jnp.where(causal, dot(head(q_ref, h), head(k_ref, h), NT), 0.0).astype(BF16)
         scores[h] = s
         local_part[h] = dot(s, head(v_ref, h), NN)
     send_totals(0)
+    for d in range(2, planes):
+        start(z_copy(d))
     spread(1)
     send_prefixes(0)
     for d in range(2, planes):
         spread(d)
+    pass_on(0)
+    loads[3].wait()
+    loads[4].wait()
     wait_state(0)
     for h in range(HEADS):
         a = (local_part[h] + dot(head(q_ref, h), state_of(0, h), NN)) * scale
         att[:, h * HEAD:(h + 1) * HEAD] = a.astype(BF16)
     for d in range(planes):
-        pass_on(d)
+        if d:
+            pass_on(d)
         reduce_1(targets[d])
+
+    half = planes // 2
+    grad_acc = jnp.zeros(att.shape, F32)
     for d in range(planes):
         pass_diag(d)
-        reduce_2(targets[d])
-
-    grad_acc = jnp.zeros(att.shape, F32)
+        if d % 2:
+            reduce_2(targets[d // 2])
     for d in range(planes):
         for i in range(4):
             sib_copy(d, i).wait_recv()
-    for i in range(planes):
-        w = full_w[i].reshape(width, w_ref.shape[1])
-        grad_acc = grad_acc + dot(cot_ref[:, i * width:(i + 1) * width], w, NN)
+        w = full_w[plane_before(d)].reshape(width, w_ref.shape[1])
+        columns = pl.ds(pl.multiple_of(plane_before(d) * width, 128), width)
+        grad_acc = grad_acc + dot(cot_ref[:, columns], w, NN)
     grad[...] = (grad_acc * scale).astype(BF16)
     pieces(1, q_ref, grad)
     send_pieces(1)
-    for d in targets:
-        reduce_3(d)
+    for d in range(half):
+        reduce_2(targets[half + d])
+        reduce_3(targets[d])
     send_totals(1)
-    for i in range(planes // 2):
+    for d in range(half, planes):
+        reduce_3(targets[d])
+
+    def mix(i):
         w = full_w[i].reshape(width, w_ref.shape[1])
         mixed_ref[:, i * width:(i + 1) * width] = dot(att[...], w, NT).astype(BF16)
+
+    mix(0)
     send_prefixes(1)
-    for d in targets:
-        reduce_4(d)
-    for i in range(planes // 2, planes):
-        w = full_w[i].reshape(width, w_ref.shape[1])
-        mixed_ref[:, i * width:(i + 1) * width] = dot(att[...], w, NT).astype(BF16)
+    for d in range(planes):
+        if d:
+            mix(d)
+        reduce_4(targets[d])
     wait_state(1)
     for h in range(HEADS):
         cols = slice(h * HEAD, (h + 1) * HEAD)
@@ -326,14 +351,24 @@
         c.wait_send()
 
 
+def place(*refs):
+    sems = refs[10]
+    copies = [pltpu.make_async_copy(refs[i], refs[5 + i], sems.at[i]) for i in range(5)]
+    for c in copies:
+        c.start()
+    for c in copies:
+        c.wait()
+
+
 def body(planes, queries, keys, values, out_weight, cotangent):
     tokens, hf = queries.shape
     rows = out_weight.shape[0]
     half = HEAD // 2
     dma = pltpu.SemaphoreType.DMA
     vmem = pl.BlockSpec(memory_space=pltpu.VMEM)
+    hbm = pl.BlockSpec(memory_space=pl.ANY)
     blocks = pltpu.VMEM((planes, rows, hf), BF16)
-    return pl.pallas_call(
+    results = pl.pallas_call(
         functools.partial(kernel, planes),
         out_shape=(
             jax.ShapeDtypeStruct(cotangent.shape, BF16),
@@ -342,9 +377,14 @@
             jax.ShapeDtypeStruct(queries.shape, BF16),
             jax.ShapeDtypeStruct(out_weight.shape, F32),
         ),
-        in_specs=[vmem] * 5,
+        in_specs=[hbm] * 5,
         out_specs=(vmem,) * 5,
         scratch_shapes=[
+            pltpu.VMEM(queries.shape, BF16),
+            pltpu.VMEM(queries.shape, BF16),
+            pltpu.VMEM(queries.shape, BF16),
+            pltpu.VMEM(cotangent.shape, BF16),
+            dma((5,)),
             pltpu.VMEM((planes, 4, 2, rows, hf), BF16),
             pltpu.VMEM((planes, 4, 2, rows, hf), BF16),
             pltpu.VMEM((planes, 4, rows, hf), BF16),
@@ -366,9 +406,17 @@
             dma((2, GROUP)), dma((2, GROUP)),
         ] + [dma((planes,))] * 8 + [dma((planes, 4))] * 2 + [dma((planes,))] * 10,
         compiler_params=pltpu.CompilerParams(
-            collective_id=0, has_side_effects=True, vmem_limit_bytes=48 * 1024 * 1024
+            collective_id=0, has_side_effects=True, vmem_limit_bytes=60 * 1024 * 1024
         ),
     )(queries, keys, values, out_weight, cotangent)
+    return pl.pallas_call(
+        place,
+        out_shape=[jax.ShapeDtypeStruct(r.shape, r.dtype) for r in results],
+        in_specs=[hbm] * 5,
+        out_specs=[hbm] * 5,
+        scratch_shapes=[dma((5,))],
+        compiler_params=pltpu.CompilerParams(vmem_limit_bytes=60 * 1024 * 1024),
+    )(*results)
 
 
 def solution(mesh):

time: 76.1 us -> 117 us (1.54)
  Pallas kernels: 66.8 us -> 117 us
  local copies, waits for them, and re-layouts: 8.47 us -> 0 us
    pallas_call x0 -> x1, Pallas kernels: none -> 52.8 us  [body(): pl.pallas_call(place, out_shape=[jax.ShapeDtypeStruct(r.shape, r.dtype) f...]
    unnamed x15 -> x0, local copies, waits for them, and re-layouts: 8.47 us -> none
    pallas_call x1, Pallas kernels: 66.8 us -> 63.8 us  [body(): pl.pallas_call(functools.partial(kernel, planes), out_shape=(jax.ShapeDty...]
where the time goes in v2:
time: 117 us
  Pallas kernels  117 us (100%)
    pallas_call x1, Pallas kernels, body(): pl.pallas_call(functools.partial(kernel, planes), out_shape=(jax.ShapeDty...  63.8 us
    pallas_call x1, Pallas kernels, body(): pl.pallas_call(place, out_shape=[jax.ShapeDtypeStruct(r.shape, r.dtype) f...  52.8 us

profile of v2, /device:TPU:0, one launch (start us, length us, event | category | flops | bytes accessed | tf_op | source)
XLA Modules:
  0.0 117.2 jit_solution(13257971990584371496)
XLA Ops:
  0.6 63.8 %shard_map.92 = (bf16[128,4096]{1,0:T(8,128)(2,1)}, bf16[128,512]{1,0:T(8,128)(2,1)}, bf16[128,512]{1,0:T(8,128)(2,1)}, bf16[128,512]{1,0:T(8,128)(2,1)}, f32[128,512]{1,0:T(8,128)}) custom-call(bf16[128,512]{1,0:T(8,128)(2,1)} %q_hbm.1, bf16[128,512]{1,0:T(8,128)(2,1)} %k_hbm.1, bf16[128,512]{1,0:T(8,128)(2,1)} %v_hbm.1, bf16[128,512]{1,0:T(8,128)(2,1)} %w_ref.1, ...), custom_call_target="tpu_custom_call" | custom-call | tf_op jit(solution)/shard_map/pallas_call | solution.py:371
  64.5 52.8 %shard_map.93 = (bf16[128,4096]{1,0:T(8,128)(2,1)}, bf16[128,512]{1,0:T(8,128)(2,1)}, bf16[128,512]{1,0:T(8,128)(2,1)}, bf16[128,512]{1,0:T(8,128)(2,1)}, f32[128,512]{1,0:T(8,128)}) custom-call(bf16[128,4096]{1,0:T(8,128)(2,1)} %get-tuple-element.10.refs_0_, bf16[128,512]{1,0:T(8,128)(2,1)} %get-tuple-element.11.refs_1_, ...), custom_call_target="tpu_custom_call" | custom-call | tf_op jit(solution)/shard_map/pallas_call | solution.py:412

commit v3 on v2

--- a/solution.py
+++ b/solution.py
@@ -27,8 +27,9 @@
 def kernel(
     planes,
     q_hbm, k_hbm, v_hbm, w_ref, cot_hbm,
-    mixed_ref, dq_ref, dk_ref, dv_ref, wg_ref,
-    q_ref, k_ref, v_ref, cot_ref, load,
+    mixed_hbm, dq_hbm, dk_hbm, dv_hbm, wg_hbm,
+    mixed_ref, dq_ref, dk_ref, dv_ref, wg_ref, store,
+    q_ref, k_ref, v_ref, cot_ref, cot_t, load,
     full_w, part, from_sib, summed, from_diag, from_x, from_y, to_plane, from_plane, own_sum,
     scores, local_part, att, grad,
     piece_out, piece_in, total_out, totals, prefix_out, state,
@@ -206,8 +207,8 @@
         return copy(part.at[d, :, other], from_sib.at[d], rs_send.at[d], rs_recv.at[d], sib)
 
     def reduce_1(d):
-        columns = pl.ds(pl.multiple_of(plane_at(d) * width, 128), width)
-        term = dot(cot_ref[:, columns], att[...], TN).astype(BF16)
+        span = pl.ds(pl.multiple_of(plane_at(d) * width, 128), width)
+        term = dot(cot_t[span, :], att[...], NN).astype(BF16)
         part[d] = term.reshape(4, 2, rows, term.shape[-1])
         start(rs_copy(d))
 
@@ -292,26 +293,31 @@
         start(z_copy(d))
     spread(1)
     send_prefixes(0)
-    for d in range(2, planes):
-        spread(d)
     pass_on(0)
     loads[3].wait()
     loads[4].wait()
+    for i in range(planes):
+        cot_t[i * width:(i + 1) * width, :] = cot_ref[:, i * width:(i + 1) * width].T
+    spread(2)
     wait_state(0)
     for h in range(HEADS):
         a = (local_part[h] + dot(head(q_ref, h), state_of(0, h), NN)) * scale
         att[:, h * HEAD:(h + 1) * HEAD] = a.astype(BF16)
-    for d in range(planes):
-        if d:
-            pass_on(d)
+    reduce_1(targets[0])
+    pass_on(1)
+    reduce_1(targets[1])
+    for d in range(3, planes):
+        spread(d)
+    for d in range(2, planes):
         reduce_1(targets[d])
+        pass_on(d)
 
     half = planes // 2
-    grad_acc = jnp.zeros(att.shape, F32)
     for d in range(planes):
         pass_diag(d)
         if d % 2:
             reduce_2(targets[d // 2])
+    grad_acc = jnp.zeros(att.shape, F32)
     for d in range(planes):
         for i in range(4):
             sib_copy(d, i).wait_recv()
@@ -321,22 +327,35 @@
     grad[...] = (grad_acc * scale).astype(BF16)
     pieces(1, q_ref, grad)
     send_pieces(1)
+
+    stores = []
+
+    def put(i, src, dst):
+        c = pltpu.make_async_copy(src, dst, store.at[i])
+        c.start()
+        stores.append(c)
+
+    def mix(i):
+        w = full_w[i].reshape(width, w_ref.shape[1])
+        cols = pl.ds(i * width, width)
+        mixed_ref[:, cols] = dot(att[...], w, NT).astype(BF16)
+        put(4 + i, mixed_ref.at[:, cols], mixed_hbm.at[:, cols])
+
     for d in range(half):
-        reduce_2(targets[half + d])
         reduce_3(targets[d])
+    for d in range(half, planes):
+        reduce_2(targets[d])
+    mix(0)
     send_totals(1)
+    for d in range(half):
+        reduce_4(targets[d])
+    mix(1)
+    send_prefixes(1)
     for d in range(half, planes):
         reduce_3(targets[d])
-
-    def mix(i):
-        w = full_w[i].reshape(width, w_ref.shape[1])
-        mixed_ref[:, i * width:(i + 1) * width] = dot(att[...], w, NT).astype(BF16)
-
-    mix(0)
-    send_prefixes(1)
-    for d in range(planes):
-        if d:
-            mix(d)
+    for i in range(2, planes):
+        mix(i)
+    for d in range(half, planes - 1):
         reduce_4(targets[d])
     wait_state(1)
     for h in range(HEADS):
@@ -346,17 +365,28 @@
         dq_ref[:, cols] = (dot(gs, k, NN) + dot(g, state_of(0, h), NT)).astype(BF16)
         dk_ref[:, cols] = (dot(gs, q, TN) + dot(v, state_of(1, h), NT)).astype(BF16)
         dv_ref[:, cols] = (dot(scores[h], g, TN) + dot(k, state_of(1, h), NN)).astype(BF16)
+    put(0, dq_ref, dq_hbm)
+    put(1, dk_ref, dk_hbm)
+    put(2, dv_ref, dv_hbm)
+    reduce_4(0)
     reduce_5()
+    put(3, wg_ref, wg_hbm)
     for c in sent:
         c.wait_send()
+    for c in stores:
+        c.wait()
 
 
 def place(*refs):
-    sems = refs[10]
-    copies = [pltpu.make_async_copy(refs[i], refs[5 + i], sems.at[i]) for i in range(5)]
-    for c in copies:
+    load, store = refs[15:]
+    loads = [pltpu.make_async_copy(refs[i], refs[10 + i], load.at[i]) for i in range(5)]
+    stores = [pltpu.make_async_copy(refs[10 + i], refs[5 + i], store.at[i]) for i in range(5)]
+    for c in loads:
         c.start()
-    for c in copies:
+    for i in range(5):
+        loads[i].wait()
+        stores[i].start()
+    for c in stores:
         c.wait()
 
 
@@ -365,7 +395,6 @@
     rows = out_weight.shape[0]
     half = HEAD // 2
     dma = pltpu.SemaphoreType.DMA
-    vmem = pl.BlockSpec(memory_space=pltpu.VMEM)
     hbm = pl.BlockSpec(memory_space=pl.ANY)
     blocks = pltpu.VMEM((planes, rows, hf), BF16)
     results = pl.pallas_call(
@@ -378,12 +407,19 @@
             jax.ShapeDtypeStruct(out_weight.shape, F32),
         ),
         in_specs=[hbm] * 5,
-        out_specs=(vmem,) * 5,
+        out_specs=(hbm,) * 5,
         scratch_shapes=[
-            pltpu.VMEM(queries.shape, BF16),
-            pltpu.VMEM(queries.shape, BF16),
-            pltpu.VMEM(queries.shape, BF16),
             pltpu.VMEM(cotangent.shape, BF16),
+            pltpu.VMEM(queries.shape, BF16),
+            pltpu.VMEM(queries.shape, BF16),
+            pltpu.VMEM(queries.shape, BF16),
+            pltpu.VMEM(out_weight.shape, F32),
+            dma((4 + planes,)),
+            pltpu.VMEM(queries.shape, BF16),
+            pltpu.VMEM(queries.shape, BF16),
+            pltpu.VMEM(queries.shape, BF16),
+            pltpu.VMEM(cotangent.shape, BF16),
+            pltpu.VMEM(cotangent.shape[::-1], BF16),
             dma((5,)),
             pltpu.VMEM((planes, 4, 2, rows, hf), BF16),
             pltpu.VMEM((planes, 4, 2, rows, hf), BF16),
@@ -414,7 +450,7 @@
         out_shape=[jax.ShapeDtypeStruct(r.shape, r.dtype) for r in results],
         in_specs=[hbm] * 5,
         out_specs=[hbm] * 5,
-        scratch_shapes=[dma((5,))],
+        scratch_shapes=[pltpu.VMEM(r.shape, r.dtype) for r in results] + [dma((5,))] * 2,
         compiler_params=pltpu.CompilerParams(vmem_limit_bytes=60 * 1024 * 1024),
     )(*results)
 

time: 117 us -> 65.7 us (0.56)
  Pallas kernels: 117 us -> 64.9 us
    pallas_call x1, Pallas kernels: 52.8 us -> 2.49 us  [body(): pl.pallas_call(place, out_shape=[jax.ShapeDtypeStruct(r.shape, r.dtype) f...]
    pallas_call x1, Pallas kernels: 63.8 us -> 62.4 us  [body(): pl.pallas_call(functools.partial(kernel, planes), out_shape=(jax.ShapeDty...]
where the time goes in v3:
time: 65.7 us; the launch traced here: 65.5 us
  Pallas kernels  64.9 us (99%)
    pallas_call x1, Pallas kernels, body(): pl.pallas_call(functools.partial(kernel, planes), out_shape=(jax.ShapeDty...  62.4 us
    pallas_call x1, Pallas kernels, body(): pl.pallas_call(place, out_shape=[jax.ShapeDtypeStruct(r.shape, r.dtype) f...  2.49 us

profile of v3, /device:TPU:0, one launch (start us, length us, event | category | flops | bytes accessed | tf_op | source)
XLA Modules:
  0.0 65.5 jit_solution(1885902103163152206)
XLA Ops:
  0.6 62.4 %shard_map.92 = (bf16[128,4096]{1,0:T(8,128)(2,1)}, bf16[128,512]{1,0:T(8,128)(2,1)}, bf16[128,512]{1,0:T(8,128)(2,1)}, bf16[128,512]{1,0:T(8,128)(2,1)}, f32[128,512]{1,0:T(8,128)}) custom-call(bf16[128,512]{1,0:T(8,128)(2,1)} %q_hbm.1, bf16[128,512]{1,0:T(8,128)(2,1)} %k_hbm.1, bf16[128,512]{1,0:T(8,128)(2,1)} %v_hbm.1, bf16[128,512]{1,0:T(8,128)(2,1)} %w_ref.1, ...), custom_call_target="tpu_custom_call" | custom-call | tf_op jit(solution)/shard_map/pallas_call | solution.py:400
  63.0 2.5 %shard_map.93 = (bf16[128,4096]{1,0:T(8,128)(2,1)}, bf16[128,512]{1,0:T(8,128)(2,1)}, bf16[128,512]{1,0:T(8,128)(2,1)}, bf16[128,512]{1,0:T(8,128)(2,1)}, f32[128,512]{1,0:T(8,128)}) custom-call(bf16[128,4096]{1,0:T(8,128)(2,1)} %get-tuple-element.10.refs_0_, bf16[128,512]{1,0:T(8,128)(2,1)} %get-tuple-element.11.refs_1_, ...), custom_call_target="tpu_custom_call" | custom-call | tf_op jit(solution)/shard_map/pallas_call | solution.py:448

commit v4 on v3

--- a/solution.py
+++ b/solution.py
@@ -30,12 +30,12 @@
     mixed_hbm, dq_hbm, dk_hbm, dv_hbm, wg_hbm,
     mixed_ref, dq_ref, dk_ref, dv_ref, wg_ref, store,
     q_ref, k_ref, v_ref, cot_ref, cot_t, load,
-    full_w, part, from_sib, summed, from_diag, from_x, from_y, to_plane, from_plane, own_sum,
+    full_w, cot_in, att_in, to_plane, from_plane, own_sum,
     scores, local_part, att, grad,
     piece_out, piece_in, total_out, totals, prefix_out, state,
     p1_send, p1_recv, p2_send, p2_recv, p3_send, p3_recv,
     z_send, z_recv, x_send, x_recv, y_send, y_recv, g_send, g_recv, s_send, s_recv,
-    rs_send, rs_recv, rd_send, rd_recv, rx_send, rx_recv, ry_send, ry_recv, rz_send, rz_recv,
+    rz_send, rz_recv, c_send, c_recv, a_send, a_recv,
 ):
     tokens = q_ref.shape[0]
     rows = w_ref.shape[0]
@@ -203,63 +203,38 @@
         diag_copy(d).wait_recv()
         start(sib_copy(d, 3))
 
-    def rs_copy(d):
-        return copy(part.at[d, :, other], from_sib.at[d], rs_send.at[d], rs_recv.at[d], sib)
-
-    def reduce_1(d):
-        span = pl.ds(pl.multiple_of(plane_at(d) * width, 128), width)
-        term = dot(cot_t[span, :], att[...], NN).astype(BF16)
-        part[d] = term.reshape(4, 2, rows, term.shape[-1])
-        start(rs_copy(d))
-
-    def rd_copy(d):
-        return copy(summed.at[d, col_d], from_diag.at[d], rd_send.at[d], rd_recv.at[d],
-                    y_dev if d % 2 else x_dev)
-
-    def rx_copy(d):
-        return copy(summed.at[d, col_x], from_x.at[d], rx_send.at[d], rx_recv.at[d], x_dev)
-
-    def ry_copy(d):
-        return copy(summed.at[d, col_y], from_y.at[d], ry_send.at[d], ry_recv.at[d], y_dev)
-
-    def reduce_2(d):
-        rs_copy(d).wait_recv()
-
-        def add(col):
-            pair = part[d, col, core].astype(F32) + from_sib[d, col].astype(F32)
-            summed[d, col] = pair.astype(BF16)
-
-        add(col_d)
-        start(rd_copy(d))
-        if d % 2:
-            add(col_y)
-            start(ry_copy(d))
-            add(col_x)
-        else:
-            add(col_x)
-            start(rx_copy(d))
-            add(col_y)
-
-    def reduce_3(d):
-        rd_copy(d).wait_recv()
-        col = col_x if d % 2 else col_y
-        both = summed[d, col].astype(F32) + from_diag[d].astype(F32)
-        summed[d, col] = both.astype(BF16)
-        start(rx_copy(d) if d % 2 else ry_copy(d))
+    def cot_copy(r):
+        return copy(cot_t.at[:, mate(r)], cot_in.at[member], c_send.at[r], c_recv.at[r], mate_dev(r))
+
+    def att_copy(i):
+        half = tokens // 2
+        col, rows_of, device = (
+            (quad, None, x_dev), (quad, None, y_dev), (quad, None, sib), (col_x, None, sib),
+            (col_x, pl.ds(half, half), y_dev), (col_y, None, sib), (col_y, pl.ds(0, half), x_dev),
+            (col_d, None, sib),
+        )[i]
+        ref = att_in.at[col, core] if rows_of is None else att_in.at[col, core, rows_of]
+        return copy(ref, ref, a_send.at[i], a_recv.at[i], device)
 
     def rz_copy(d):
         return copy(to_plane.at[d], from_plane.at[d], rz_send.at[d], rz_recv.at[d], plane_dev(d))
 
-    def reduce_4(d):
-        rx_copy(d).wait_recv()
-        ry_copy(d).wait_recv()
-        pair = part[d, quad, core].astype(F32) + from_sib[d, quad].astype(F32)
-        total = pair + from_x[d].astype(F32) + from_y[d].astype(F32)
-        if d:
-            to_plane[d] = total.astype(BF16)
-            start(rz_copy(d))
-        else:
-            own_sum[...] = total
+    def reduce_plane():
+        for r in range(1, GROUP):
+            cot_copy(r).wait_recv()
+        for i in (2, 3, 5, 7):
+            att_copy(i).wait_recv()
+        tall = jnp.concatenate([
+            jnp.concatenate([cot_in[j, plane_at(d)] for j in range(GROUP)], axis=1) for d in targets
+        ], axis=0)
+        total = dot(tall, att_in[...].reshape(GROUP * tokens, HEADS * HEAD), NN)
+        for i, d in enumerate(targets):
+            block_sum = total[i * rows:(i + 1) * rows]
+            if d:
+                to_plane[d] = block_sum.astype(BF16)
+                start(rz_copy(d))
+            else:
+                own_sum[...] = block_sum
 
     def reduce_5():
         total = own_sum[...]
@@ -291,32 +266,43 @@
     send_totals(0)
     for d in range(2, planes):
         start(z_copy(d))
+    loads[4].wait()
+    for i in range(planes):
+        cot_t[i] = cot_ref[:, i * width:(i + 1) * width].T.reshape(GROUP, rows, tokens)
+    for r in range(1, 4):
+        start(cot_copy(r))
     spread(1)
     send_prefixes(0)
+    for r in range(4, GROUP):
+        start(cot_copy(r))
+    cot_in[member] = cot_t[:, member]
     pass_on(0)
+    spread(2)
     loads[3].wait()
-    loads[4].wait()
-    for i in range(planes):
-        cot_t[i * width:(i + 1) * width, :] = cot_ref[:, i * width:(i + 1) * width].T
-    spread(2)
     wait_state(0)
     for h in range(HEADS):
         a = (local_part[h] + dot(head(q_ref, h), state_of(0, h), NN)) * scale
         att[:, h * HEAD:(h + 1) * HEAD] = a.astype(BF16)
-    reduce_1(targets[0])
+    att_in[quad, core] = att[...]
+    for i in range(3):
+        start(att_copy(i))
     pass_on(1)
-    reduce_1(targets[1])
     for d in range(3, planes):
         spread(d)
+    att_copy(0).wait_recv()
+    start(att_copy(4))
+    start(att_copy(3))
+    att_copy(1).wait_recv()
+    start(att_copy(6))
+    start(att_copy(5))
     for d in range(2, planes):
-        reduce_1(targets[d])
         pass_on(d)
-
-    half = planes // 2
+    att_copy(4).wait_recv()
+    att_copy(6).wait_recv()
+    start(att_copy(7))
     for d in range(planes):
         pass_diag(d)
-        if d % 2:
-            reduce_2(targets[d // 2])
+    reduce_plane()
     grad_acc = jnp.zeros(att.shape, F32)
     for d in range(planes):
         for i in range(4):
@@ -341,22 +327,14 @@
         mixed_ref[:, cols] = dot(att[...], w, NT).astype(BF16)
         put(4 + i, mixed_ref.at[:, cols], mixed_hbm.at[:, cols])
 
-    for d in range(half):
-        reduce_3(targets[d])
-    for d in range(half, planes):
-        reduce_2(targets[d])
-    mix(0)
+    half = planes // 2
+    for i in range(half):
+        mix(i)
     send_totals(1)
-    for d in range(half):
-        reduce_4(targets[d])
-    mix(1)
+    mix(half)
     send_prefixes(1)
-    for d in range(half, planes):
-        reduce_3(targets[d])
-    for i in range(2, planes):
+    for i in range(half + 1, planes):
         mix(i)
-    for d in range(half, planes - 1):
-        reduce_4(targets[d])
     wait_state(1)
     for h in range(HEADS):
         cols = slice(h * HEAD, (h + 1) * HEAD)
@@ -368,7 +346,6 @@
     put(0, dq_ref, dq_hbm)
     put(1, dk_ref, dk_hbm)
     put(2, dv_ref, dv_hbm)
-    reduce_4(0)
     reduce_5()
     put(3, wg_ref, wg_hbm)
     for c in sent:
@@ -419,13 +396,12 @@
             pltpu.VMEM(queries.shape, BF16),
             pltpu.VMEM(queries.shape, BF16),
             pltpu.VMEM(cotangent.shape, BF16),
-            pltpu.VMEM(cotangent.shape[::-1], BF16),
+            pltpu.VMEM((planes, GROUP, rows, tokens), BF16),
             dma((5,)),
             pltpu.VMEM((planes, 4, 2, rows, hf), BF16),
-            pltpu.VMEM((planes, 4, 2, rows, hf), BF16),
-            pltpu.VMEM((planes, 4, rows, hf), BF16),
-            pltpu.VMEM((planes, 4, rows, hf), BF16),
-            blocks, blocks, blocks, blocks, blocks,
+            pltpu.VMEM((GROUP, planes, rows, tokens), BF16),
+            pltpu.VMEM((4, 2, tokens, hf), BF16),
+            blocks, blocks,
             pltpu.VMEM((rows, hf), F32),
             pltpu.VMEM((HEADS, tokens, tokens), BF16),
             pltpu.VMEM((HEADS, tokens, HEAD), F32),
@@ -440,7 +416,7 @@
             dma((2, GROUP)), dma((2, GROUP)),
             dma((2, planes)), dma((2, planes)),
             dma((2, GROUP)), dma((2, GROUP)),
-        ] + [dma((planes,))] * 8 + [dma((planes, 4))] * 2 + [dma((planes,))] * 10,
+        ] + [dma((planes,))] * 8 + [dma((planes, 4))] * 2 + [dma((planes,))] * 2 + [dma((GROUP,))] * 4,
         compiler_params=pltpu.CompilerParams(
             collective_id=0, has_side_effects=True, vmem_limit_bytes=60 * 1024 * 1024
         ),

time: 65.7 us -> 69.1 us (1.052)
  Pallas kernels: 64.9 us -> 68.3 us
    pallas_call x1, Pallas kernels: 62.4 us -> 65.8 us  [body(): pl.pallas_call(functools.partial(kernel, planes), out_shape=(jax.ShapeDty...]
where the time goes in v4:
time: 69.1 us; the launch traced here: 68.9 us
  Pallas kernels  68.3 us (99%)
    pallas_call x1, Pallas kernels, body(): pl.pallas_call(functools.partial(kernel, planes), out_shape=(jax.ShapeDty...  65.8 us
    pallas_call x1, Pallas kernels, body(): pl.pallas_call(place, out_shape=[jax.ShapeDtypeStruct(r.shape, r.dtype) f...  2.49 us

profile of v4, /device:TPU:0, one launch (start us, length us, event | category | flops | bytes accessed | tf_op | source)
XLA Modules:
  0.0 68.9 jit_solution(10315149267307239289)
XLA Ops:
  0.6 65.8 %shard_map.92 = (bf16[128,4096]{1,0:T(8,128)(2,1)}, bf16[128,512]{1,0:T(8,128)(2,1)}, bf16[128,512]{1,0:T(8,128)(2,1)}, bf16[128,512]{1,0:T(8,128)(2,1)}, f32[128,512]{1,0:T(8,128)}) custom-call(bf16[128,512]{1,0:T(8,128)(2,1)} %q_hbm.1, bf16[128,512]{1,0:T(8,128)(2,1)} %k_hbm.1, bf16[128,512]{1,0:T(8,128)(2,1)} %v_hbm.1, bf16[128,512]{1,0:T(8,128)(2,1)} %w_ref.1, ...), custom_call_target="tpu_custom_call" | custom-call | tf_op jit(solution)/shard_map/pallas_call | solution.py:377
  66.4 2.5 %shard_map.93 = (bf16[128,4096]{1,0:T(8,128)(2,1)}, bf16[128,512]{1,0:T(8,128)(2,1)}, bf16[128,512]{1,0:T(8,128)(2,1)}, bf16[128,512]{1,0:T(8,128)(2,1)}, f32[128,512]{1,0:T(8,128)}) custom-call(bf16[128,4096]{1,0:T(8,128)(2,1)} %get-tuple-element.10.refs_0_, bf16[128,512]{1,0:T(8,128)(2,1)} %get-tuple-element.11.refs_1_, ...), custom_call_target="tpu_custom_call" | custom-call | tf_op jit(solution)/shard_map/pallas_call | solution.py:424

commit v5 on v3

--- a/solution.py
+++ b/solution.py
@@ -30,12 +30,13 @@
     mixed_hbm, dq_hbm, dk_hbm, dv_hbm, wg_hbm,
     mixed_ref, dq_ref, dk_ref, dv_ref, wg_ref, store,
     q_ref, k_ref, v_ref, cot_ref, cot_t, load,
-    full_w, part, from_sib, summed, from_diag, from_x, from_y, to_plane, from_plane, own_sum,
+    cot_sib, cot_sel, att_pair, att_sib, grad_sib, grad_in, dk_part, dv_part,
+    full_w, summed, from_diag, from_x, from_y, to_plane, from_plane, own_sum,
     scores, local_part, att, grad,
     piece_out, piece_in, total_out, totals, prefix_out, state,
     p1_send, p1_recv, p2_send, p2_recv, p3_send, p3_recv,
     z_send, z_recv, x_send, x_recv, y_send, y_recv, g_send, g_recv, s_send, s_recv,
-    rs_send, rs_recv, rd_send, rd_recv, rx_send, rx_recv, ry_send, ry_recv, rz_send, rz_recv,
+    e_send, e_recv, rd_send, rd_recv, rx_send, rx_recv, ry_send, ry_recv, rz_send, rz_recv,
 ):
     tokens = q_ref.shape[0]
     rows = w_ref.shape[0]
@@ -203,14 +204,12 @@
         diag_copy(d).wait_recv()
         start(sib_copy(d, 3))
 
-    def rs_copy(d):
-        return copy(part.at[d, :, other], from_sib.at[d], rs_send.at[d], rs_recv.at[d], sib)
-
-    def reduce_1(d):
-        span = pl.ds(pl.multiple_of(plane_at(d) * width, 128), width)
-        term = dot(cot_t[span, :], att[...], NN).astype(BF16)
-        part[d] = term.reshape(4, 2, rows, term.shape[-1])
-        start(rs_copy(d))
+    exchanges = [
+        copy(src, dst, e_send.at[i], e_recv.at[i], sib)
+        for i, (src, dst) in enumerate((
+            (cot_t.at[:, :, other], cot_sib), (att, att_sib), (grad_sib, grad_in),
+        ))
+    ]
 
     def rd_copy(d):
         return copy(summed.at[d, col_d], from_diag.at[d], rd_send.at[d], rd_recv.at[d],
@@ -223,22 +222,12 @@
         return copy(summed.at[d, col_y], from_y.at[d], ry_send.at[d], ry_recv.at[d], y_dev)
 
     def reduce_2(d):
-        rs_copy(d).wait_recv()
-
-        def add(col):
-            pair = part[d, col, core].astype(F32) + from_sib[d, col].astype(F32)
-            summed[d, col] = pair.astype(BF16)
-
-        add(col_d)
+        a = plane_at(d)
+        tall = jnp.concatenate([cot_t[a, :, core], cot_sib[a]], axis=-1)
+        term = dot(tall.reshape(4 * rows, 2 * tokens), att_pair[...], NN).astype(BF16)
+        summed[d] = term.reshape(4, rows, HEADS * HEAD)
         start(rd_copy(d))
-        if d % 2:
-            add(col_y)
-            start(ry_copy(d))
-            add(col_x)
-        else:
-            add(col_x)
-            start(rx_copy(d))
-            add(col_y)
+        start(ry_copy(d) if d % 2 else rx_copy(d))
 
     def reduce_3(d):
         rd_copy(d).wait_recv()
@@ -253,8 +242,7 @@
     def reduce_4(d):
         rx_copy(d).wait_recv()
         ry_copy(d).wait_recv()
-        pair = part[d, quad, core].astype(F32) + from_sib[d, quad].astype(F32)
-        total = pair + from_x[d].astype(F32) + from_y[d].astype(F32)
+        total = summed[d, quad].astype(F32) + from_x[d].astype(F32) + from_y[d].astype(F32)
         if d:
             to_plane[d] = total.astype(BF16)
             start(rz_copy(d))
@@ -291,40 +279,47 @@
     send_totals(0)
     for d in range(2, planes):
         start(z_copy(d))
+    loads[4].wait()
+    for i in range(planes):
+        cot_t[i] = cot_ref[:, i * width:(i + 1) * width].T.reshape(4, 2, rows, tokens)
+    start(exchanges[0])
     spread(1)
     send_prefixes(0)
+    for i in range(planes):
+        cot_sel[i, :tokens] = cot_t[i, :, core].reshape(4 * rows, tokens).T
     pass_on(0)
+    spread(2)
     loads[3].wait()
-    loads[4].wait()
-    for i in range(planes):
-        cot_t[i * width:(i + 1) * width, :] = cot_ref[:, i * width:(i + 1) * width].T
-    spread(2)
     wait_state(0)
     for h in range(HEADS):
         a = (local_part[h] + dot(head(q_ref, h), state_of(0, h), NN)) * scale
         att[:, h * HEAD:(h + 1) * HEAD] = a.astype(BF16)
-    reduce_1(targets[0])
+    start(exchanges[1])
     pass_on(1)
-    reduce_1(targets[1])
     for d in range(3, planes):
         spread(d)
+    att_pair[:tokens] = att[...]
+    exchanges[0].wait_recv()
+    for i in range(planes):
+        cot_sel[i, tokens:] = cot_sib[i].reshape(4 * rows, tokens).T
     for d in range(2, planes):
-        reduce_1(targets[d])
         pass_on(d)
+    exchanges[1].wait_recv()
+    att_pair[tokens:] = att_sib[...]
 
     half = planes // 2
+    for d in range(half):
+        reduce_2(targets[d])
+    grad_acc = jnp.zeros((2 * tokens, HEADS * HEAD), F32)
     for d in range(planes):
         pass_diag(d)
-        if d % 2:
-            reduce_2(targets[d // 2])
-    grad_acc = jnp.zeros(att.shape, F32)
-    for d in range(planes):
-        for i in range(4):
-            sib_copy(d, i).wait_recv()
-        w = full_w[plane_before(d)].reshape(width, w_ref.shape[1])
-        columns = pl.ds(pl.multiple_of(plane_before(d) * width, 128), width)
-        grad_acc = grad_acc + dot(cot_ref[:, columns], w, NN)
-    grad[...] = (grad_acc * scale).astype(BF16)
+        w = full_w[plane_before(d), :, core].reshape(4 * rows, HEADS * HEAD)
+        grad_acc = grad_acc + dot(cot_sel[plane_before(d)], w, NN)
+    grad_sib[...] = grad_acc[tokens:]
+    start(exchanges[2])
+    own_grad = grad_acc[:tokens]
+    exchanges[2].wait_recv()
+    grad[...] = ((own_grad + grad_in[...]) * scale).astype(BF16)
     pieces(1, q_ref, grad)
     send_pieces(1)
 
@@ -345,29 +340,37 @@
         reduce_3(targets[d])
     for d in range(half, planes):
         reduce_2(targets[d])
-    mix(0)
     send_totals(1)
+    for h in range(HEADS):
+        cols = slice(h * HEAD, (h + 1) * HEAD)
+        q, k, v, g = head(q_ref, h), head(k_ref, h), head(v_ref, h), head(grad, h)
+        gs = jnp.where(causal, dot(g, v, NT), 0.0).astype(BF16)
+        dq_ref[:, cols] = (dot(gs, k, NN) + dot(g, state_of(0, h), NT)).astype(BF16)
+        dk_part[:, cols] = dot(gs, q, TN)
+        dv_part[:, cols] = dot(scores[h], g, TN)
+    send_prefixes(1)
+    put(0, dq_ref, dq_hbm)
     for d in range(half):
         reduce_4(targets[d])
-    mix(1)
-    send_prefixes(1)
     for d in range(half, planes):
         reduce_3(targets[d])
-    for i in range(2, planes):
+    for d in range(planes):
+        for i in range(4):
+            sib_copy(d, i).wait_recv()
+    for i in range(half):
         mix(i)
     for d in range(half, planes - 1):
         reduce_4(targets[d])
     wait_state(1)
     for h in range(HEADS):
         cols = slice(h * HEAD, (h + 1) * HEAD)
-        q, k, v, g = head(q_ref, h), head(k_ref, h), head(v_ref, h), head(grad, h)
-        gs = jnp.where(causal, dot(g, v, NT), 0.0).astype(BF16)
-        dq_ref[:, cols] = (dot(gs, k, NN) + dot(g, state_of(0, h), NT)).astype(BF16)
-        dk_ref[:, cols] = (dot(gs, q, TN) + dot(v, state_of(1, h), NT)).astype(BF16)
-        dv_ref[:, cols] = (dot(scores[h], g, TN) + dot(k, state_of(1, h), NN)).astype(BF16)
-    put(0, dq_ref, dq_hbm)
+        k, v = head(k_ref, h), head(v_ref, h)
+        dk_ref[:, cols] = (dk_part[:, cols] + dot(v, state_of(1, h), NT)).astype(BF16)
+        dv_ref[:, cols] = (dv_part[:, cols] + dot(k, state_of(1, h), NN)).astype(BF16)
     put(1, dk_ref, dk_hbm)
     put(2, dv_ref, dv_hbm)
+    for i in range(half, planes):
+        mix(i)
     reduce_4(0)
     reduce_5()
     put(3, wg_ref, wg_hbm)
@@ -419,11 +422,17 @@
             pltpu.VMEM(queries.shape, BF16),
             pltpu.VMEM(queries.shape, BF16),
             pltpu.VMEM(cotangent.shape, BF16),
-            pltpu.VMEM(cotangent.shape[::-1], BF16),
+            pltpu.VMEM((planes, 4, 2, rows, tokens), BF16),
             dma((5,)),
+            pltpu.VMEM((planes, 4, rows, tokens), BF16),
+            pltpu.VMEM((planes, 2 * tokens, 4 * rows), BF16),
+            pltpu.VMEM((2 * tokens, hf), BF16),
+            pltpu.VMEM((tokens, hf), BF16),
+            pltpu.VMEM((tokens, hf), F32),
+            pltpu.VMEM((tokens, hf), F32),
+            pltpu.VMEM((tokens, hf), F32),
+            pltpu.VMEM((tokens, hf), F32),
             pltpu.VMEM((planes, 4, 2, rows, hf), BF16),
-            pltpu.VMEM((planes, 4, 2, rows, hf), BF16),
-            pltpu.VMEM((planes, 4, rows, hf), BF16),
             pltpu.VMEM((planes, 4, rows, hf), BF16),
             blocks, blocks, blocks, blocks, blocks,
             pltpu.VMEM((rows, hf), F32),
@@ -440,7 +449,7 @@
             dma((2, GROUP)), dma((2, GROUP)),
             dma((2, planes)), dma((2, planes)),
             dma((2, GROUP)), dma((2, GROUP)),
-        ] + [dma((planes,))] * 8 + [dma((planes, 4))] * 2 + [dma((planes,))] * 10,
+        ] + [dma((planes,))] * 8 + [dma((planes, 4))] * 2 + [dma((3,))] * 2 + [dma((planes,))] * 8,
         compiler_params=pltpu.CompilerParams(
             collective_id=0, has_side_effects=True, vmem_limit_bytes=60 * 1024 * 1024
         ),

time: 65.7 us -> 64.8 us (0.986)
  Pallas kernels: 64.9 us -> 64 us
    pallas_call x1, Pallas kernels: 62.4 us -> 61.5 us  [body(): pl.pallas_call(functools.partial(kernel, planes), out_shape=(jax.ShapeDty...]
where the time goes in v5:
time: 64.8 us; the launch traced here: 64.6 us
  Pallas kernels  64 us (99%)
    pallas_call x1, Pallas kernels, body(): pl.pallas_call(functools.partial(kernel, planes), out_shape=(jax.ShapeDty...  61.5 us
    pallas_call x1, Pallas kernels, body(): pl.pallas_call(place, out_shape=[jax.ShapeDtypeStruct(r.shape, r.dtype) f...  2.49 us

profile of v5, /device:TPU:0, one launch (start us, length us, event | category | flops | bytes accessed | tf_op | source)
XLA Modules:
  0.0 64.6 jit_solution(13615345636958070914)
XLA Ops:
  0.6 61.5 %shard_map.92 = (bf16[128,4096]{1,0:T(8,128)(2,1)}, bf16[128,512]{1,0:T(8,128)(2,1)}, bf16[128,512]{1,0:T(8,128)(2,1)}, bf16[128,512]{1,0:T(8,128)(2,1)}, f32[128,512]{1,0:T(8,128)}) custom-call(bf16[128,512]{1,0:T(8,128)(2,1)} %q_hbm.1, bf16[128,512]{1,0:T(8,128)(2,1)} %k_hbm.1, bf16[128,512]{1,0:T(8,128)(2,1)} %v_hbm.1, bf16[128,512]{1,0:T(8,128)(2,1)} %w_ref.1, ...), custom_call_target="tpu_custom_call" | custom-call | tf_op jit(solution)/shard_map/pallas_call | solution.py:403
  62.2 2.5 %shard_map.93 = (bf16[128,4096]{1,0:T(8,128)(2,1)}, bf16[128,512]{1,0:T(8,128)(2,1)}, bf16[128,512]{1,0:T(8,128)(2,1)}, bf16[128,512]{1,0:T(8,128)(2,1)}, f32[128,512]{1,0:T(8,128)}) custom-call(bf16[128,4096]{1,0:T(8,128)(2,1)} %get-tuple-element.10.refs_0_, bf16[128,512]{1,0:T(8,128)(2,1)} %get-tuple-element.11.refs_1_, ...), custom_call_target="tpu_custom_call" | custom-call | tf_op jit(solution)/shard_map/pallas_call | solution.py:457

commit v6 on v5

--- a/solution.py
+++ b/solution.py
@@ -256,7 +256,8 @@
             total = total + from_plane[d].astype(F32)
         wg_ref[...] = total
 
-    targets = list(range(1, planes)) + [0]
+    targets = list(range(2, planes)) + [1, 0]
+    sources = [0, 1] + list(range(planes - 1, 1, -1))
 
     position = me * tokens + lax.broadcasted_iota(jnp.int32, (tokens, 1), 0)
     scale = lax.rsqrt(HEAD * (position + 1).astype(F32))
@@ -277,7 +278,7 @@
         scores[h] = s
         local_part[h] = dot(s, head(v_ref, h), NN)
     send_totals(0)
-    for d in range(2, planes):
+    for d in sources[2:]:
         start(z_copy(d))
     loads[4].wait()
     for i in range(planes):
@@ -288,7 +289,7 @@
     for i in range(planes):
         cot_sel[i, :tokens] = cot_t[i, :, core].reshape(4 * rows, tokens).T
     pass_on(0)
-    spread(2)
+    spread(sources[2])
     loads[3].wait()
     wait_state(0)
     for h in range(HEADS):
@@ -296,13 +297,13 @@
         att[:, h * HEAD:(h + 1) * HEAD] = a.astype(BF16)
     start(exchanges[1])
     pass_on(1)
-    for d in range(3, planes):
+    for d in sources[3:]:
         spread(d)
     att_pair[:tokens] = att[...]
     exchanges[0].wait_recv()
     for i in range(planes):
         cot_sel[i, tokens:] = cot_sib[i].reshape(4 * rows, tokens).T
-    for d in range(2, planes):
+    for d in sources[2:]:
         pass_on(d)
     exchanges[1].wait_recv()
     att_pair[tokens:] = att_sib[...]
@@ -311,7 +312,7 @@
     for d in range(half):
         reduce_2(targets[d])
     grad_acc = jnp.zeros((2 * tokens, HEADS * HEAD), F32)
-    for d in range(planes):
+    for d in sources:
         pass_diag(d)
         w = full_w[plane_before(d), :, core].reshape(4 * rows, HEADS * HEAD)
         grad_acc = grad_acc + dot(cot_sel[plane_before(d)], w, NN)
@@ -357,8 +358,7 @@
     for d in range(planes):
         for i in range(4):
             sib_copy(d, i).wait_recv()
-    for i in range(half):
-        mix(i)
+    mix(0)
     for d in range(half, planes - 1):
         reduce_4(targets[d])
     wait_state(1)
@@ -369,7 +369,7 @@
         dv_ref[:, cols] = (dv_part[:, cols] + dot(k, state_of(1, h), NN)).astype(BF16)
     put(1, dk_ref, dk_hbm)
     put(2, dv_ref, dv_hbm)
-    for i in range(half, planes):
+    for i in range(1, planes):
         mix(i)
     reduce_4(0)
     reduce_5()

time: 64.8 us -> 64 us (0.988)
  Pallas kernels: 64 us -> 63.2 us
    pallas_call x1, Pallas kernels: 61.5 us -> 60.7 us  [body(): pl.pallas_call(functools.partial(kernel, planes), out_shape=(jax.ShapeDty...]
where the time goes in v6:
time: 64 us; the launch traced here: 63.8 us
  Pallas kernels  63.2 us (99%)
  between operations  0.64 us (1%)
    pallas_call x1, Pallas kernels, body(): pl.pallas_call(functools.partial(kernel, planes), out_shape=(jax.ShapeDty...  60.7 us
    pallas_call x1, Pallas kernels, body(): pl.pallas_call(place, out_shape=[jax.ShapeDtypeStruct(r.shape, r.dtype) f...  2.49 us

profile of v6, /device:TPU:0, one launch (start us, length us, event | category | flops | bytes accessed | tf_op | source)
XLA Modules:
  0.0 63.8 jit_solution(5322698429717878882)
XLA Ops:
  0.6 60.7 %shard_map.92 = (bf16[128,4096]{1,0:T(8,128)(2,1)}, bf16[128,512]{1,0:T(8,128)(2,1)}, bf16[128,512]{1,0:T(8,128)(2,1)}, bf16[128,512]{1,0:T(8,128)(2,1)}, f32[128,512]{1,0:T(8,128)}) custom-call(bf16[128,512]{1,0:T(8,128)(2,1)} %q_hbm.1, bf16[128,512]{1,0:T(8,128)(2,1)} %k_hbm.1, bf16[128,512]{1,0:T(8,128)(2,1)} %v_hbm.1, bf16[128,512]{1,0:T(8,128)(2,1)} %w_ref.1, ...), custom_call_target="tpu_custom_call" | custom-call | tf_op jit(solution)/shard_map/pallas_call | solution.py:403
  61.3 2.5 %shard_map.93 = (bf16[128,4096]{1,0:T(8,128)(2,1)}, bf16[128,512]{1,0:T(8,128)(2,1)}, bf16[128,512]{1,0:T(8,128)(2,1)}, bf16[128,512]{1,0:T(8,128)(2,1)}, f32[128,512]{1,0:T(8,128)}) custom-call(bf16[128,4096]{1,0:T(8,128)(2,1)} %get-tuple-element.10.refs_0_, bf16[128,512]{1,0:T(8,128)(2,1)} %get-tuple-element.11.refs_1_, ...), custom_call_target="tpu_custom_call" | custom-call | tf_op jit(solution)/shard_map/pallas_call | solution.py:457

commit v7 on v6

--- a/solution.py
+++ b/solution.py
@@ -311,14 +311,18 @@
     half = planes // 2
     for d in range(half):
         reduce_2(targets[d])
+    ahead = targets[half:]
     grad_acc = jnp.zeros((2 * tokens, HEADS * HEAD), F32)
     for d in sources:
         pass_diag(d)
         w = full_w[plane_before(d), :, core].reshape(4 * rows, HEADS * HEAD)
         grad_acc = grad_acc + dot(cot_sel[plane_before(d)], w, NN)
+        if ahead:
+            reduce_2(ahead.pop(0))
     grad_sib[...] = grad_acc[tokens:]
     start(exchanges[2])
     own_grad = grad_acc[:tokens]
+    reduce_3(targets[0])
     exchanges[2].wait_recv()
     grad[...] = ((own_grad + grad_in[...]) * scale).astype(BF16)
     pieces(1, q_ref, grad)
@@ -337,11 +341,12 @@
         mixed_ref[:, cols] = dot(att[...], w, NT).astype(BF16)
         put(4 + i, mixed_ref.at[:, cols], mixed_hbm.at[:, cols])
 
-    for d in range(half):
+    for d in range(1, half):
         reduce_3(targets[d])
+    reduce_4(targets[0])
+    send_totals(1)
     for d in range(half, planes):
-        reduce_2(targets[d])
-    send_totals(1)
+        reduce_3(targets[d])
     for h in range(HEADS):
         cols = slice(h * HEAD, (h + 1) * HEAD)
         q, k, v, g = head(q_ref, h), head(k_ref, h), head(v_ref, h), head(grad, h)
@@ -351,10 +356,8 @@
         dv_part[:, cols] = dot(scores[h], g, TN)
     send_prefixes(1)
     put(0, dq_ref, dq_hbm)
-    for d in range(half):
+    for d in range(1, half):
         reduce_4(targets[d])
-    for d in range(half, planes):
-        reduce_3(targets[d])
     for d in range(planes):
         for i in range(4):
             sib_copy(d, i).wait_recv()

time: 64 us -> 71 us (1.11)
  the two profiles are of different devices: /device:TPU:0 before, /device:TPU:4 now
where the time goes in v7:
time: 71 us; the launch traced here: 70.9 us
  Pallas kernels  70.2 us (99%)
    pallas_call x1, Pallas kernels, body(): pl.pallas_call(functools.partial(kernel, planes), out_shape=(jax.ShapeDty...  67.7 us
    pallas_call x1, Pallas kernels, body(): pl.pallas_call(place, out_shape=[jax.ShapeDtypeStruct(r.shape, r.dtype) f...  2.49 us

profile of v7, /device:TPU:4, one launch (start us, length us, event | category | flops | bytes accessed | tf_op | source)
XLA Modules:
  0.0 70.9 jit_solution(6091197225620687628)
XLA Ops:
  0.6 67.7 %shard_map.92 = (bf16[128,4096]{1,0:T(8,128)(2,1)}, bf16[128,512]{1,0:T(8,128)(2,1)}, bf16[128,512]{1,0:T(8,128)(2,1)}, bf16[128,512]{1,0:T(8,128)(2,1)}, f32[128,512]{1,0:T(8,128)}) custom-call(bf16[128,512]{1,0:T(8,128)(2,1)} %q_hbm.1, bf16[128,512]{1,0:T(8,128)(2,1)} %k_hbm.1, bf16[128,512]{1,0:T(8,128)(2,1)} %v_hbm.1, bf16[128,512]{1,0:T(8,128)(2,1)} %w_ref.1, ...), custom_call_target="tpu_custom_call" | custom-call | tf_op jit(solution)/shard_map/pallas_call | solution.py:406
  68.4 2.5 %shard_map.93 = (bf16[128,4096]{1,0:T(8,128)(2,1)}, bf16[128,512]{1,0:T(8,128)(2,1)}, bf16[128,512]{1,0:T(8,128)(2,1)}, bf16[128,512]{1,0:T(8,128)(2,1)}, f32[128,512]{1,0:T(8,128)}) custom-call(bf16[128,4096]{1,0:T(8,128)(2,1)} %get-tuple-element.10.refs_0_, bf16[128,512]{1,0:T(8,128)(2,1)} %get-tuple-element.11.refs_1_, ...), custom_call_target="tpu_custom_call" | custom-call | tf_op jit(solution)/shard_map/pallas_call | solution.py:460

commit v8 on v6

--- a/solution.py
+++ b/solution.py
@@ -309,8 +309,6 @@
     att_pair[tokens:] = att_sib[...]
 
     half = planes // 2
-    for d in range(half):
-        reduce_2(targets[d])
     grad_acc = jnp.zeros((2 * tokens, HEADS * HEAD), F32)
     for d in sources:
         pass_diag(d)
@@ -319,6 +317,8 @@
     grad_sib[...] = grad_acc[tokens:]
     start(exchanges[2])
     own_grad = grad_acc[:tokens]
+    for d in range(half):
+        reduce_2(targets[d])
     exchanges[2].wait_recv()
     grad[...] = ((own_grad + grad_in[...]) * scale).astype(BF16)
     pieces(1, q_ref, grad)
@@ -339,8 +339,6 @@
 
     for d in range(half):
         reduce_3(targets[d])
-    for d in range(half, planes):
-        reduce_2(targets[d])
     send_totals(1)
     for h in range(HEADS):
         cols = slice(h * HEAD, (h + 1) * HEAD)
@@ -350,6 +348,8 @@
         dk_part[:, cols] = dot(gs, q, TN)
         dv_part[:, cols] = dot(scores[h], g, TN)
     send_prefixes(1)
+    for d in range(half, planes):
+        reduce_2(targets[d])
     put(0, dq_ref, dq_hbm)
     for d in range(half):
         reduce_4(targets[d])

time: 64 us -> 70.1 us (1.095)
  Pallas kernels: 63.2 us -> 69.3 us
    pallas_call x1, Pallas kernels: 60.7 us -> 66.8 us  [body(): pl.pallas_call(functools.partial(kernel, planes), out_shape=(jax.ShapeDty...]
where the time goes in v8:
time: 70.1 us; the launch traced here: 69.9 us
  Pallas kernels  69.3 us (99%)
    pallas_call x1, Pallas kernels, body(): pl.pallas_call(functools.partial(kernel, planes), out_shape=(jax.ShapeDty...  66.8 us
    pallas_call x1, Pallas kernels, body(): pl.pallas_call(place, out_shape=[jax.ShapeDtypeStruct(r.shape, r.dtype) f...  2.49 us

profile of v8, /device:TPU:0, one launch (start us, length us, event | category | flops | bytes accessed | tf_op | source)
XLA Modules:
  0.0 69.9 jit_solution(5916701056832117086)
XLA Ops:
  0.6 66.8 %shard_map.92 = (bf16[128,4096]{1,0:T(8,128)(2,1)}, bf16[128,512]{1,0:T(8,128)(2,1)}, bf16[128,512]{1,0:T(8,128)(2,1)}, bf16[128,512]{1,0:T(8,128)(2,1)}, f32[128,512]{1,0:T(8,128)}) custom-call(bf16[128,512]{1,0:T(8,128)(2,1)} %q_hbm.1, bf16[128,512]{1,0:T(8,128)(2,1)} %k_hbm.1, bf16[128,512]{1,0:T(8,128)(2,1)} %v_hbm.1, bf16[128,512]{1,0:T(8,128)(2,1)} %w_ref.1, ...), custom_call_target="tpu_custom_call" | custom-call | tf_op jit(solution)/shard_map/pallas_call | solution.py:403
  67.4 2.5 %shard_map.93 = (bf16[128,4096]{1,0:T(8,128)(2,1)}, bf16[128,512]{1,0:T(8,128)(2,1)}, bf16[128,512]{1,0:T(8,128)(2,1)}, bf16[128,512]{1,0:T(8,128)(2,1)}, f32[128,512]{1,0:T(8,128)}) custom-call(bf16[128,4096]{1,0:T(8,128)(2,1)} %get-tuple-element.10.refs_0_, bf16[128,512]{1,0:T(8,128)(2,1)} %get-tuple-element.11.refs_1_, ...), custom_call_target="tpu_custom_call" | custom-call | tf_op jit(solution)/shard_map/pallas_call | solution.py:457
